TPU v7x, 32 devices: a whole 2x2x4 slice. The times are simulated.
32 devices in a mesh: inline: 16 (over z, y, x), xline: 2 (over core).
Axes of the slice: x: 2, y: 2, z: 4, core: 2. Of those that a mesh axis runs over, the one named last changes fastest.
Arguments:
- source_field: bfloat16 [4, 2, 2048, 128], P(None, 'xline', 'inline'), may hold values from -6 to 6
- receiver_field: bfloat16 [4, 2, 2048, 128], P(None, 'xline', 'inline'), may hold values from -6 to 6
- sat_mask: int32 [2, 2048, 128], P('xline', 'inline'), may hold values 0 or 1
- offset_range: int32 [16], P('inline'), may hold values from 8 to 32, as said below
Outputs:
- source_adjoint: bfloat16 [4, 2, 2048, 128], P(None, 'xline', 'inline')
- receiver_adjoint: bfloat16 [4, 2, 2048, 128], P(None, 'xline', 'inline')
- semblance: float32 [], replicated
Inputs may be any that keep to these rules, and one draw needn't show every extreme that they name: `offset_range`: some slab has exactly 32.
All inputs are finite; a program needn't handle non-finite values. No bound on the sum of `sat_mask` on one device may be relied on, other than what follows from the above.
Results may differ from a plain program's by a relative error of at most 0.00075.
Values may be sent and summed in bfloat16 or wider, within the bound.
No kernel may reach another device: no remote copies, remote signals or barrier semaphores. Data moves between devices by JAX's collectives and lax.ppermute only.
A program may use at most 64 MiB of HBM per device.

v0:
```python
import jax
import jax.numpy as jnp
from jax import lax
from jax.sharding import PartitionSpec as P

H = 32
BLOCK = 13


EPSILON = 1e-06
SATURATION = 0.25


def extended(value, sides, width):
    for axis, dim in sides:
        size, length = (lax.axis_size(axis), value.shape[dim])
        up = [(i, (i + 1) % size) for i in range(size - 1)]
        down = [(j, i) for i, j in up]
        last = lax.slice_in_dim(value, length - width, length, axis=dim)
        first = lax.slice_in_dim(value, 0, width, axis=dim)
        before = lax.ppermute(last, axis, up)
        after = lax.ppermute(first, axis, down)
        value = jnp.concatenate([before, value, after], axis=dim)
    return value


def shifted(block, axis, distance):
    devices = range(lax.axis_size(axis))
    route = [(i - distance, i) for i in devices if i - distance in devices]
    return lax.ppermute(block, axis, route)


def local(source_field, receiver_field, sat_mask, offset_range):
    inline_cells = source_field.shape[2]
    stacked = jnp.stack([source_field, receiver_field])
    padded = extended(stacked, (("inline", 3),), H)
    src_ext = padded[0]
    rcv_ext = padded[1]
    reach_limit = offset_range[0]
    saturated = sat_mask != 0
    cell_count = float(
        sat_mask.shape[0]
        * lax.axis_size("xline")
        * inline_cells
        * lax.axis_size("inline")
        * sat_mask.shape[2]
        * (2 * H + 1)
    )
    zero = jnp.zeros((), jnp.float32)
    block_starts = jnp.arange(0, 2 * H + 1, BLOCK, dtype=jnp.int32) - H

    def image_at(offset):
        src_window = lax.dynamic_slice_in_dim(src_ext, H - offset, inline_cells, 2)
        rcv_window = lax.dynamic_slice_in_dim(rcv_ext, H + offset, inline_cells, 2)
        inside = (jnp.abs(offset) <= reach_limit).astype(jnp.float32)
        product = jnp.sum(src_window.astype(jnp.float32) * rcv_window.astype(jnp.float32), axis=0)
        return (product * inside, src_window, rcv_window)

    def weight_square(offset):
        relative = offset.astype(jnp.float32) / H
        squared = relative * relative
        weight = jnp.where(saturated, jnp.minimum(squared, SATURATION), squared)
        return weight * weight

    def add_into(buffer, addend, anchor):
        section = lax.dynamic_slice_in_dim(buffer, anchor, inline_cells, 2)
        return lax.dynamic_update_slice_in_dim(buffer, section + addend, anchor, 2)

    ext_shape = (src_ext.shape[0], src_ext.shape[1], src_ext.shape[2], src_ext.shape[3])
    empty = jnp.zeros(ext_shape, jnp.float32)

    def joint_block(running, start):
        energy, weighted, src_heavy, src_plain, rcv_heavy, rcv_plain = running
        for inner in range(BLOCK):
            offset = start + inner
            image, src_window, rcv_window = image_at(offset)
            heavy_image = weight_square(offset) * image
            energy = energy + jnp.sum(image * image)
            weighted = weighted + jnp.sum(heavy_image * image)
            rcv_values = rcv_window.astype(jnp.float32)
            src_values = src_window.astype(jnp.float32)
            src_anchor = H - offset
            rcv_anchor = H + offset
            src_heavy = add_into(src_heavy, heavy_image[None] * rcv_values, src_anchor)
            src_plain = add_into(src_plain, image[None] * rcv_values, src_anchor)
            rcv_heavy = add_into(rcv_heavy, heavy_image[None] * src_values, rcv_anchor)
            rcv_plain = add_into(rcv_plain, image[None] * src_values, rcv_anchor)
        return ((energy, weighted, src_heavy, src_plain, rcv_heavy, rcv_plain), None)

    start_state = (zero, zero, empty, empty, empty, empty)
    (energy, weighted, src_heavy, src_plain, rcv_heavy, rcv_plain), _ = lax.scan(
        joint_block, start_state, block_starts
    )
    global_energy = energy
    global_weighted = weighted
    global_energy, global_weighted = lax.psum((global_energy, global_weighted), ("inline", "xline"))
    semblance = global_weighted / global_energy
    inverse_rms = 1.0 / jnp.sqrt(global_energy / cell_count + EPSILON)
    buffers = (src_heavy, src_plain, rcv_heavy, rcv_plain)
    lower_rims = jnp.stack([member[:, :, :H] for member in buffers])
    upper_rims = jnp.stack([member[:, :, H + inline_cells :] for member in buffers])
    from_above = shifted(lower_rims, "inline", -1)
    from_below = shifted(upper_rims, "inline", 1)
    results = []
    for position in range(len(buffers)):
        interior = buffers[position][:, :, H : H + inline_cells]
        interior = interior.at[:, :, inline_cells - H :].add(from_above[position])
        interior = interior.at[:, :, :H].add(from_below[position])
        results.append(interior)
    src_adj = inverse_rms * (results[0] - semblance * results[1])
    rcv_adj = inverse_rms * (results[2] - semblance * results[3])
    return (src_adj.astype(jnp.bfloat16), rcv_adj.astype(jnp.bfloat16), semblance)


def solution(mesh):
    return jax.shard_map(
        local,
        mesh=mesh,
        in_specs=(
            P(None, "xline", "inline", None),
            P(None, "xline", "inline", None),
            P("xline", "inline", None),
            P("inline"),
        ),
        out_specs=(P(None, "xline", "inline", None), P(None, "xline", "inline", None), P()),
        check_vma=False,
    )
```

profile of v0, /device:TPU:0, one launch (start us, length us, event | category | flops | bytes accessed | tf_op | source)
XLA Modules:
  0.0 539.1 jit_solution(5887041712048817052)
XLA Ops:
  0.7 0.9 pad_maximum_fusion.4
  1.5 4.8 collective-permute-start
  6.4 1.3 collective-permute-start.1
  8.3 4.2 collective-permute-done.1
  12.8 465.6 %while.33 = (s32[]{:T(128)}, f32[]{:T(128)}, f32[]{:T(128)}, f32[4,1,192,128]{3,2,1,0:T(8,128)S(1)}, f32[4,1,192,128]{3,2,1,0:T(8,128)S(1)}, /*index=5*/f32[4,1,...) while((s32[]{:T(128)}, f32[]{:T(128)}, f32[]{:T(128)}, ...), condition=%wide.region_40.41_spmd, body=%wide.region_0.40_spmd.sunk | while | flops 15761617 | bytes 73437224 | solution.py:91
  12.8 1.3 dynamic_slice.1026
  51.2 1.2 fusion.112
  55.7 0.8 multiply_reduce_fusion.28
  106.0 1.3 dynamic_slice.1026
  144.4 1.2 fusion.112
  148.9 0.8 multiply_reduce_fusion.28
  199.2 1.3 dynamic_slice.1026
  237.6 1.2 fusion.112
  242.1 0.8 multiply_reduce_fusion.28
  292.4 1.3 dynamic_slice.1026
  330.8 1.2 fusion.112
  335.3 0.8 multiply_reduce_fusion.28
  385.4 1.3 dynamic_slice.1026
  423.8 1.1 fusion.112
  428.3 0.8 multiply_reduce_fusion.28
  478.4 1.3 collective-permute-start.2
  479.8 7.8 %collective-permute-done.2 = f32[4,4,1,32,128]{4,3,1,2,0:T(8,128)S(1)} collective-permute-done((f32[4,4,1,32,128]{4,3,1,2,0:T(8,128)S(1)}, f32[4,4,1,32,128]{4,3,1,2,0:T(8,128)S(1)}, u32[]{:S(2)}, u32[]{:S(2)}) %collective-permute-start.2) | collective-permute-done | bytes 262176 | tf_op jit(solution)/shard_map/ppermute | solution.py:30
  487.6 4.6 collective-permute-start.3
  492.2 42.2 %all-reduce = (f32[]{:T(128)}, f32[]{:T(128)}) all-reduce(f32[]{:T(128)} %get-tuple-element.451, f32[]{:T(128)} %get-tuple-element.446), channel_id=1, replica_groups=mesh['inline'=16,'xline'=2] {'inline','xline'}, use_global_device_ids=true, to_apply=%region_42.43 | all-reduce | flops 2 | bytes 16 | tf_op jit(solution)/shard_map/psum | solution.py:96
  (540 shorter events, 191.1 us)
Async XLA Ops:
  0.6 7.1 %copy-start.12 = (s32[1,128,128]{2,1,0:T(8,128)S(1)}, s32[1,128,128]{2,1,0:T(8,128)}, u32[]{:S(2)}) copy-start(s32[1,128,128]{2,1,0:T(8,128)} %param.24) | copy-start | bytes 196612
  0.6 11.9 %copy-start.10 = (bf16[4,1,128,128]{3,2,1,0:T(8,128)(2,1)S(1)}, bf16[4,1,128,128]{3,2,1,0:T(8,128)(2,1)}, u32[]{:S(2)}) copy-start(bf16[4,1,128,128]{3,2,1,0:T(8,128)(2,1)} %param.23) | copy-start | bytes 393220
  0.7 11.9 %copy-start.11 = (bf16[4,1,128,128]{3,2,1,0:T(8,128)(2,1)S(1)}, bf16[4,1,128,128]{3,2,1,0:T(8,128)(2,1)}, u32[]{:S(2)}) copy-start(bf16[4,1,128,128]{3,2,1,0:T(8,128)(2,1)} %param.22) | copy-start | bytes 393220
  1.5 6.8 %collective-permute-start = (bf16[2,4,1,32,128]{4,3,1,2,0:T(8,128)(2,1)S(1)}, bf16[2,4,1,32,128]{4,3,1,2,0:T(8,128)(2,1)S(1)}, u32[]{:S(2)}, u32[]{:S(2)}) collective-permute-start(bf16[2,4,1,32,128]{4,3,1,2,0:T(8,128)(2,1)S(1)} %get-tuple-element.658), channel_id=1, source_target_pairs={{0,2},{2,4},{4,6},{6,8},{8,10},{10,12},{12,14},{14,16},{16,18},{18... | collective-permute-start | bytes 196616 | tf_op jit(solution)/shard_map/ppermute | solution.py:21
  6.4 6.2 %collective-permute-start.1 = (bf16[2,4,1,32,128]{4,3,1,2,0:T(8,128)(2,1)S(1)}, bf16[2,4,1,32,128]{4,3,1,2,0:T(8,128)(2,1)S(1)}, u32[]{:S(2)}, u32[]{:S(2)}) collective-permute-start(bf16[2,4,1,32,128]{4,3,1,2,0:T(8,128)(2,1)S(1)} %get-tuple-element.659), channel_id=1, source_target_pairs={{2,0},{4,2},{6,4},{8,6},{10,8},{12,10},{14,12},{16,14},{18,16},{20... | collective-permute-start | bytes 196616 | tf_op jit(solution)/shard_map/ppermute | solution.py:22
  84.3 0.8 copy-start.7
  86.9 0.8 copy-start.9
  88.5 0.8 copy-start.3
  90.0 0.8 copy-start.8
  93.1 0.8 copy-start.5
  177.6 0.8 copy-start.7
  181.8 0.8 copy-start.3
  186.4 0.8 copy-start.5
  194.8 0.8 copy-start
  270.8 0.8 copy-start.7
  275.1 0.8 copy-start.3
  279.6 0.8 copy-start.5
  364.0 0.8 copy-start.7
  368.2 0.8 copy-start.3
  379.6 0.8 copy-start.1
  457.1 0.8 copy-start.7
  461.3 0.8 copy-start.3
  478.4 9.2 %collective-permute-start.2 = (f32[4,4,1,32,128]{4,3,1,2,0:T(8,128)S(1)}, f32[4,4,1,32,128]{4,3,1,2,0:T(8,128)S(1)}, u32[]{:S(2)}, u32[]{:S(2)}) collective-permute-start(f32[4,4,1,32,128]{4,3,1,2,0:T(8,128)S(1)} %pad_maximum_fusion.1), channel_id=1, source_target_pairs={{2,0},{4,2},{6,4},{8,6},{10,8},{12,10},{14,12},{16,14},{18,16},{20... | collective-permute-start | bytes 786440 | tf_op jit(solution)/shard_map/ppermute | solution.py:30
  487.6 48.8 %collective-permute-start.3 = (f32[4,4,1,32,128]{4,3,1,2,0:T(8,128)S(1)}, f32[4,4,1,32,128]{4,3,1,2,0:T(8,128)S(1)}, u32[]{:S(2)}, u32[]{:S(2)}) collective-permute-start(f32[4,4,1,32,128]{4,3,1,2,0:T(8,128)S(1)} %pad_maximum_fusion.2), channel_id=1, source_target_pairs={{0,2},{2,4},{4,6},{6,8},{8,10},{10,12},{12,14},{14,16},{16,18},{18... | collective-permute-start | bytes 786440 | tf_op jit(solution)/shard_map/ppermute | solution.py:30
  (33 other events, 27.7 us)
where the time goes:
time: 545 us; the launch traced here: 539 us
  loops' own time  261 us (48%)
  local copies, waits for them, and re-layouts  156 us (29%)
  other arithmetic  52.3 us (10%)
  blocking collectives  42.2 us (8%)
  starting transfers between devices  12 us (2%)
  waiting for transfers between devices  12 us (2%)
    another operation x1, loops' own time, local(): lax.scan(joint_block, start_state, block_starts)  261 us
    dynamic_update_slice x260, local copies, waits for them, and re-layouts, add_into(): return lax.dynamic_update_slice_in_dim(buffer, section + addend, anchor, 2)  133 us
    psum x1, blocking collectives, local(): lax.psum((global_energy, global_weighted), ('inline', 'xline'))  42.2 us
    add x120, other arithmetic, add_into(): return lax.dynamic_update_slice_in_dim(buffer, section + addend, anchor, 2)  18.4 us
    while x100, local copies, waits for them, and re-layouts  15.6 us
    mul x20, other arithmetic, joint_block(): heavy_image = weight_square(offset) * image  14 us
  transfers between devices with their start and end apart: 4, of which 2 were waited for; matrix products, arithmetic and copies ran while one was open for 0% of the time, Pallas kernels for 0%

commit v1 on v0

v1 whole, which is shorter than its diff:
```python
import functools

import jax
import jax.numpy as jnp
from jax import lax
from jax.experimental import pallas as pl
from jax.experimental.pallas import tpu as pltpu
from jax.sharding import PartitionSpec as P

H = 32
EPSILON = 1e-06
SATURATION = 0.25
REACH = 2 * H
ALWAYS = 8
ROWS = 8
LIMIT_ROWS = 16
VMEM = pl.BlockSpec(memory_space=pltpu.VMEM)
SMEM = pl.BlockSpec(memory_space=pltpu.SMEM)


def square_weight(offset):
    relative = (offset / H) ** 2
    return relative * relative


def payload_layout(times, lines):
    fields = 2 * times * lines * REACH
    return fields, fields + lines * H, fields + lines * H + LIMIT_ROWS


def pack_kernel(scalars, src, rcv, sat, even_out, odd_out):
    times, lines, cells, depth = src.shape
    mask_at, limit_at, _ = payload_layout(times, lines)
    parity = scalars[0]
    limit = jnp.full((LIMIT_ROWS, depth), scalars[1], jnp.int32).astype(jnp.float32).astype(jnp.bfloat16)

    def fill(out, first):
        start = 0 if first else cells - REACH
        mask_start = 0 if first else cells - H
        for position, field in enumerate((src, rcv)):
            for t in range(times):
                for y in range(lines):
                    at = ((position * times + t) * lines + y) * REACH
                    out[pl.ds(at, REACH), :] = field[t, y, pl.ds(start, REACH), :]
        for y in range(lines):
            out[pl.ds(mask_at + y * H, H), :] = (
                (sat[y, pl.ds(mask_start, H), :] != 0).astype(jnp.float32).astype(jnp.bfloat16)
            )
        out[pl.ds(limit_at, LIMIT_ROWS), :] = limit

    @pl.when(parity == 0)
    def _():
        fill(even_out, False)
        fill(odd_out, True)

    @pl.when(parity != 0)
    def _():
        fill(even_out, True)
        fill(odd_out, False)


def unpack(scalars, src, rcv, sat, even_in, odd_in, fields, masks, limits):
    times, lines, cells, depth = src.shape
    mask_at, limit_at, _ = payload_layout(times, lines)
    parity = scalars[0]

    def halo(arrived, low):
        field_at = 0 if low else REACH + cells
        row_at = 0 if low else H + cells
        for position in range(2):
            for t in range(times):
                for y in range(lines):
                    at = ((position * times + t) * lines + y) * REACH
                    fields[position, t, y, pl.ds(field_at, REACH), :] = arrived[pl.ds(at, REACH), :].astype(jnp.float32)
        limit = arrived[pl.ds(limit_at, LIMIT_ROWS), :].astype(jnp.float32)
        for y in range(lines):
            masks[y, pl.ds(row_at, H), :] = arrived[pl.ds(mask_at + y * H, H), :].astype(jnp.float32)
        for part in range(H // LIMIT_ROWS):
            limits[pl.ds(row_at + part * LIMIT_ROWS, LIMIT_ROWS), :] = limit

    @pl.when(parity == 0)
    def _():
        halo(even_in, False)
        halo(odd_in, True)

    @pl.when(parity != 0)
    def _():
        halo(even_in, True)
        halo(odd_in, False)

    for position, field in enumerate((src, rcv)):
        for t in range(times):
            for y in range(lines):
                fields[position, t, y, pl.ds(REACH, cells), :] = field[t, y].astype(jnp.float32)
    for y in range(lines):
        masks[y, pl.ds(H, cells), :] = (sat[y] != 0).astype(jnp.float32)
    limits[pl.ds(H, cells), :] = jnp.full((cells, depth), scalars[1], jnp.int32).astype(jnp.float32)


def cell(center, fields, other, limits, y, base, offset):
    times = len(center)
    far = [fields[other, t, y, pl.ds(base + REACH + 2 * offset, ROWS), :] for t in range(times)]
    image = center[0] * far[0]
    for t in range(1, times):
        image = image + center[t] * far[t]
    if abs(offset) > ALWAYS:
        limit = limits[pl.ds(base + H + offset, ROWS), :]
        image = jnp.where(limit >= float(abs(offset)), image, 0.0)
    return image, far


def weigh(image, masks, y, base, offset):
    square = square_weight(offset)
    if square <= SATURATION * SATURATION:
        return image * square
    mask = masks[y, pl.ds(base + H + offset, ROWS), :]
    return image * jnp.where(mask != 0.0, SATURATION * SATURATION, square)


def energy_kernel(scalars, src, rcv, sat, even_in, odd_in, out, fields, masks, limits):
    unpack(scalars, src, rcv, sat, even_in, odd_in, fields, masks, limits)
    times, lines, cells, depth = src.shape
    zero = jnp.zeros((ROWS, depth), jnp.float32)

    def tile(index, sums):
        energy, weighted = sums
        base = pl.multiple_of(index * ROWS, ROWS)
        for y in range(lines):
            center = [fields[0, t, y, pl.ds(base + REACH, ROWS), :] for t in range(times)]
            for offset in range(-H, H + 1):
                image, _ = cell(center, fields, 1, limits, y, base, offset)
                power = image * image
                energy = energy + power
                weighted = weighted + weigh(power, masks, y, base, offset)
        return energy, weighted

    energy, weighted = lax.fori_loop(0, cells // ROWS, tile, (zero, zero))
    out[0:1, :] = jnp.full((1, depth), jnp.sum(energy), jnp.float32)
    out[1:2, :] = jnp.full((1, depth), jnp.sum(weighted), jnp.float32)


def adjoint_kernel(scalars, src, rcv, sat, even_in, odd_in, out, fields, masks, limits):
    unpack(scalars, src, rcv, sat, even_in, odd_in, fields, masks, limits)
    times, lines, cells, depth = src.shape
    zero = jnp.zeros((ROWS, depth), jnp.float32)

    for position in range(2):
        for y in range(lines):

            def tile(index, carry):
                base = pl.multiple_of(index * ROWS, ROWS)
                center = [fields[position, t, y, pl.ds(base + REACH, ROWS), :] for t in range(times)]
                heavy, plain = [zero] * times, [zero] * times
                for offset in range(-H, H + 1):
                    image, far = cell(center, fields, 1 - position, limits, y, base, offset)
                    weighed = weigh(image, masks, y, base, offset)
                    for t in range(times):
                        plain[t] = plain[t] + image * far[t]
                        heavy[t] = heavy[t] + weighed * far[t]
                for t in range(times):
                    out[position, 0, t, y, pl.ds(base, ROWS), :] = heavy[t]
                    out[position, 1, t, y, pl.ds(base, ROWS), :] = plain[t]
                return carry

            lax.fori_loop(0, cells // ROWS, tile, 0)


def combine_kernel(cell_count, sums, parts, src_out, rcv_out, semblance_out):
    total = jnp.sum(sums[...], axis=0)
    energy, weighted = total[0:1], total[1:2]
    semblance = weighted / energy
    inverse_rms = 1.0 / jnp.sqrt(energy / cell_count + EPSILON)
    semblance_out[...] = semblance
    _, _, times, lines, _, _ = parts.shape
    for position, out in enumerate((src_out, rcv_out)):
        for t in range(times):
            for y in range(lines):
                value = inverse_rms * (parts[position, 0, t, y] - semblance * parts[position, 1, t, y])
                out[t, y] = value.astype(jnp.bfloat16)


def exchanges(size):
    even = [(i, i + 1) for i in range(0, size - 1, 2)]
    odd = [(i, i + 1) for i in range(1, size - 1, 2)]
    return [pairs + [(j, i) for i, j in pairs] for pairs in (even, odd)]


def local(source_field, receiver_field, sat_mask, offset_range):
    times, lines, cells, depth = source_field.shape
    size = lax.axis_size("inline")
    scalars = jnp.stack([lax.axis_index("inline").astype(jnp.int32) % 2, offset_range[0]])
    rows = payload_layout(times, lines)[2]
    payload = jax.ShapeDtypeStruct((rows, depth), jnp.bfloat16)
    even, odd = pl.pallas_call(
        pack_kernel,
        out_shape=(payload, payload),
        in_specs=[SMEM, VMEM, VMEM, VMEM],
        out_specs=(VMEM, VMEM),
        name="pack",
    )(scalars, source_field, receiver_field, sat_mask)
    even_route, odd_route = exchanges(size)
    even_in = lax.ppermute(even, "inline", even_route)
    odd_in = lax.ppermute(odd, "inline", odd_route)

    operands = (scalars, source_field, receiver_field, sat_mask, even_in, odd_in)
    scratch = [
        pltpu.VMEM((2, times, lines, cells + 2 * REACH, depth), jnp.float32),
        pltpu.VMEM((lines, cells + 2 * H, depth), jnp.float32),
        pltpu.VMEM((cells + 2 * H, depth), jnp.float32),
    ]
    image_cells = lines * cells * depth * (2 * H + 1)
    sums = pl.pallas_call(
        energy_kernel,
        out_shape=jax.ShapeDtypeStruct((2, depth), jnp.float32),
        in_specs=[SMEM] + [VMEM] * 5,
        out_specs=VMEM,
        scratch_shapes=scratch,
        cost_estimate=pl.CostEstimate(flops=14 * image_cells, bytes_accessed=1 << 20, transcendentals=0),
        name="energy",
    )(*operands)
    gathered = lax.all_gather(sums, ("inline", "xline"))
    parts = pl.pallas_call(
        adjoint_kernel,
        out_shape=jax.ShapeDtypeStruct((2, 2, times, lines, cells, depth), jnp.float32),
        in_specs=[SMEM] + [VMEM] * 5,
        out_specs=VMEM,
        scratch_shapes=scratch,
        cost_estimate=pl.CostEstimate(flops=54 * image_cells, bytes_accessed=1 << 22, transcendentals=0),
        name="adjoint",
    )(*operands)
    cell_count = float(lines * lax.axis_size("xline") * cells * size * depth * (2 * H + 1))
    field_out = jax.ShapeDtypeStruct(source_field.shape, jnp.bfloat16)
    src_adj, rcv_adj, semblance = pl.pallas_call(
        functools.partial(combine_kernel, cell_count),
        out_shape=(field_out, field_out, jax.ShapeDtypeStruct((1, depth), jnp.float32)),
        in_specs=[VMEM, VMEM],
        out_specs=(VMEM, VMEM, VMEM),
        name="combine",
    )(gathered, parts)
    return src_adj, rcv_adj, semblance[0, 0]


def solution(mesh):
    return jax.shard_map(
        local,
        mesh=mesh,
        in_specs=(
            P(None, "xline", "inline", None),
            P(None, "xline", "inline", None),
            P("xline", "inline", None),
            P("inline"),
        ),
        out_specs=(P(None, "xline", "inline", None), P(None, "xline", "inline", None), P()),
        check_vma=False,
    )
```

time: 545 us -> 76.5 us (0.14); the launches traced: 539 us -> 76.2 us
  loops' own time: 261 us -> 0 us
  local copies, waits for them, and re-layouts: 156 us -> 1.99 us
  other arithmetic: 52.3 us -> 0.59 us
  Pallas kernels: 0 us -> 19.7 us
  waiting for transfers between devices: 12 us -> 3.3 us
  starting transfers between devices: 12 us -> 3.6 us
    another operation x1 -> x0, loops' own time: 261 us -> none  [local(): lax.scan(joint_block, start_state, block_starts)]
    dynamic_update_slice x260 -> x0, local copies, waits for them, and re-layouts: 133 us -> none  [add_into(): return lax.dynamic_update_slice_in_dim(buffer, section + addend, anchor, 2)]
    all_gather x0 -> x1, blocking collectives: none -> 45.7 us  [local(): gathered = lax.all_gather(sums, ('inline', 'xline'))]
    psum x1 -> x0, blocking collectives: 42.2 us -> none  [local(): lax.psum((global_energy, global_weighted), ('inline', 'xline'))]
    pallas_call x0 -> x4, Pallas kernels: none -> 19.7 us  [the longest x1 11.8 us: local(): pl.pallas_call(adjoint_kernel, out_shape=jax.ShapeDtypeStruct((2, 2, time...]
    add x120 -> x0, other arithmetic: 18.4 us -> none  [add_into(): return lax.dynamic_update_slice_in_dim(buffer, section + addend, anchor, 2)]
    reduce_sum x20 -> x0, other arithmetic: 16.9 us -> none  [the longest x10 9.24 us: image_at(): jnp.sum(src_window.astype(jnp.float32) * rcv_window.astype(jnp.float32),...]
    while x100 -> x0, local copies, waits for them, and re-layouts: 15.6 us -> none
  transfers between devices with their start and end apart: 4 -> 2, of which waited for: 2 -> 1; matrix products, arithmetic and copies ran while one was open for 0% -> 0% of each run, Pallas kernels for 0% -> 0%
where the time goes in v1:
time: 76.5 us; the launch traced here: 76.2 us
  blocking collectives  45.7 us (60%)
  Pallas kernels  19.7 us (26%)
  starting transfers between devices  3.6 us (5%)
  waiting for transfers between devices  3.3 us (4%)
  local copies, waits for them, and re-layouts  1.99 us (3%)
  between operations  1.3 us (2%)
    all_gather x1, blocking collectives, local(): gathered = lax.all_gather(sums, ('inline', 'xline'))  45.7 us
    pallas_call x1, Pallas kernels, local(): pl.pallas_call(adjoint_kernel, out_shape=jax.ShapeDtypeStruct((2, 2, time...  11.8 us
    pallas_call x1, Pallas kernels, local(): pl.pallas_call(energy_kernel, out_shape=jax.ShapeDtypeStruct((2, depth),...  4.19 us
    ppermute x1, waiting for transfers between devices, local(): even_in = lax.ppermute(even, 'inline', even_route)  3.3 us
    ppermute x1, starting transfers between devices, local(): even_in = lax.ppermute(even, 'inline', even_route)  2.94 us
    pallas_call x1, Pallas kernels, local(): pl.pallas_call(functools.partial(combine_kernel, cell_count), out_shape=(...  2.02 us
    unnamed x6, local copies, waits for them, and re-layouts  1.99 us
    pallas_call x1, Pallas kernels, local(): pl.pallas_call(pack_kernel, out_shape=(payload, payload), in_specs=[SMEM,...  1.71 us
  transfers between devices with their start and end apart: 2, of which 1 were waited for; matrix products, arithmetic and copies ran while one was open for 0% of the time, Pallas kernels for 0%

profile of v1, /device:TPU:0, one launch (start us, length us, event | category | flops | bytes accessed | tf_op | source)
XLA Modules:
  0.0 76.2 jit_solution(6808824291992501404)
XLA Ops:
  1.3 0.6 pad_add_fusion.scalars
  1.9 1.7 %pack.1 = (bf16[560,128]{1,0:T(8,128)(2,1)}, bf16[560,128]{1,0:T(8,128)(2,1)}) custom-call(s32[2]{0:T(128)} %pad_add_fusion.scalars, bf16[4,1,128,128]{3,2,1,0:T(8,128)(2,1)} %src.5, bf16[4,1,128,128]{3,2,1,0:T(8,128)(2,1)} %rcv.5, s32[1,128,128]{2,1,0:T(8,128)} %sat.5), custom_call_target="tpu_custom_call" | custom-call | tf_op jit(solution)/shard_map/pack/pallas_call | solution.py:194
  3.6 2.9 %collective-permute-start = (bf16[560,128]{1,0:T(8,128)(2,1)}, bf16[560,128]{1,0:T(8,128)(2,1)S(1)}, u32[]{:S(2)}, u32[]{:S(2)}) collective-permute-start(bf16[560,128]{1,0:T(8,128)(2,1)} %get-tuple-element.8), channel_id=1, source_target_pairs={{0,2},{4,6},{8,10},{12,14},{16,18},{20,22},{24,26},{28,30},{2,0},{... | collective-permute-start | bytes 430088 | tf_op jit(solution)/shard_map/ppermute | solution.py:202
  6.5 0.7 collective-permute-start.1
  7.2 3.3 %collective-permute-done.even_in = bf16[560,128]{1,0:T(8,128)(2,1)S(1)} collective-permute-done((bf16[560,128]{1,0:T(8,128)(2,1)}, bf16[560,128]{1,0:T(8,128)(2,1)S(1)}, u32[]{:S(2)}, u32[]{:S(2)}) %collective-permute-start) | collective-permute-done | bytes 143392 | tf_op jit(solution)/shard_map/ppermute | solution.py:202
  10.5 0.0 copy-start
  10.5 0.0 collective-permute-done.1.odd_in
  10.5 0.7 copy-done
  11.2 0.0 copy-start.1
  11.2 0.7 copy-done.1
  11.8 4.2 %energy.1 = f32[2,128]{1,0:T(2,128)} custom-call(s32[2]{0:T(128)} %pad_add_fusion.scalars, bf16[4,1,128,128]{3,2,1,0:T(8,128)(2,1)} %src.5, bf16[4,1,128,128]{3,2,1,0:T(8,128)(2,1)} %rcv.5, s32[1,128,128]{2,1,0:T(8,128)} %sat.5, bf16[560,128]{1,0:T(8,128)(2,1)} %copy-done, bf16[560,128]{1,0:T(8,128)(2,1)} %copy-done.1), custom_call_target="tpu_custom_call" | custom-call | flops 14909440 | bytes 1048576 | tf_op jit(solution)/shard_map/energy/pallas_call | solution.py:212
  16.0 0.0 copy-start.2
  16.0 0.7 copy-done.2
  16.7 45.7 %all-gather.1.sums = f32[32,2,128]{2,1,0:T(2,128)} all-gather(f32[1,2,128]{2,1,0:T(2,128)S(1)} %bitcast.4), channel_id=2, replica_groups=mesh['inline'=16,'xline'=2] {'inline','xline'}, dimensions={0}, use_global_device_ids=true | all-gather | bytes 33792 | tf_op jit(solution)/shard_map/all_gather | solution.py:221
  62.4 11.8 %adjoint.1.parts = f32[2,2,4,1,128,128]{5,4,3,2,1,0:T(8,128)} custom-call(s32[2]{0:T(128)} %pad_add_fusion.scalars, bf16[4,1,128,128]{3,2,1,0:T(8,128)(2,1)} %src.5, bf16[4,1,128,128]{3,2,1,0:T(8,128)(2,1)} %rcv.5, s32[1,128,128]{2,1,0:T(8,128)} %sat.5, bf16[560,128]{1,0:T(8,128)(2,1)} %copy-done, bf16[560,128]{1,0:T(8,128)(2,1)} %copy-done.1), custom_call_target="tpu_custom_call" | custom-call | flops 57507840 | bytes 4194304 | tf_op jit(solution)/shard_map/adjoint/pallas_call | solution.py:222
  74.2 2.0 %combine.1 = (bf16[4,1,128,128]{3,2,1,0:T(8,128)(2,1)}, bf16[4,1,128,128]{3,2,1,0:T(8,128)(2,1)}, f32[1,128]{1,0:T(1,128)}) custom-call(f32[32,2,128]{2,1,0:T(2,128)} %all-gather.1.sums, f32[2,2,4,1,128,128]{5,4,3,2,1,0:T(8,128)} %adjoint.1.parts), custom_call_target="tpu_custom_call" | custom-call | tf_op jit(solution)/shard_map/combine/pallas_call | solution.py:233
Async XLA Ops:
  3.6 6.9 %collective-permute-start = (bf16[560,128]{1,0:T(8,128)(2,1)}, bf16[560,128]{1,0:T(8,128)(2,1)S(1)}, u32[]{:S(2)}, u32[]{:S(2)}) collective-permute-start(bf16[560,128]{1,0:T(8,128)(2,1)} %get-tuple-element.8), channel_id=1, source_target_pairs={{0,2},{4,6},{8,10},{12,14},{16,18},{20,22},{24,26},{28,30},{2,0},{... | collective-permute-start | bytes 430088 | tf_op jit(solution)/shard_map/ppermute | solution.py:202
  6.5 4.0 %collective-permute-start.1 = (bf16[560,128]{1,0:T(8,128)(2,1)}, bf16[560,128]{1,0:T(8,128)(2,1)S(1)}, u32[]{:S(2)}, u32[]{:S(2)}) collective-permute-start(bf16[560,128]{1,0:T(8,128)(2,1)} %get-tuple-element.9), channel_id=1, source_target_pairs={{2,4},{6,8},{10,12},{14,16},{18,20},{22,24},{26,28},{4,2},{8,6},{1... | collective-permute-start | bytes 430088 | tf_op jit(solution)/shard_map/ppermute | solution.py:203
  10.5 0.7 copy-start
  11.2 0.7 copy-start.1
  16.0 0.7 copy-start.2

commit v2 on v1

v2 whole, which is shorter than its diff:
```python
import functools

import jax
import jax.numpy as jnp
from jax import lax
from jax.experimental import pallas as pl
from jax.experimental.pallas import tpu as pltpu
from jax.sharding import PartitionSpec as P

H = 32
EPSILON = 1e-06
SATURATION = 0.25
REACH = 2 * H
ALWAYS = 8
SHARED = H // 2
ROWS = 8
PAIR = 2 * ROWS
LIMIT_ROWS = 16
PIECES = 4
GRANT = 12 << 20
VMEM = pl.BlockSpec(memory_space=pltpu.VMEM)
SMEM = pl.BlockSpec(memory_space=pltpu.SMEM)


def square_weight(offset):
    relative = (offset / H) ** 2
    return relative * relative


def payload_layout(times, lines):
    mask_at = 2 * times * lines * REACH
    limit_at = mask_at + lines * H
    return mask_at, limit_at, limit_at + LIMIT_ROWS


def by_parity(even, odd, work):
    parity = lax.rem(lax.axis_index("inline"), 2)

    @pl.when(parity == 0)
    def _():
        work(even, False)
        work(odd, True)

    @pl.when(parity != 0)
    def _():
        work(even, True)
        work(odd, False)


def payloads(src, rcv, sat, limit):
    cells, depth = src.shape[2:]

    def rows(low):
        start, mask_start = (0, 0) if low else (cells - REACH, cells - H)
        fields = [lax.slice_in_dim(field, start, start + REACH, axis=2).reshape(-1, depth) for field in (src, rcv)]
        mask = lax.slice_in_dim(sat, mask_start, mask_start + H, axis=1).reshape(-1, depth)
        marks = [(mask != 0).astype(jnp.bfloat16), jnp.full((LIMIT_ROWS, depth), limit[0]).astype(jnp.bfloat16)]
        return jnp.concatenate(fields + marks, axis=0)

    low, high = rows(True), rows(False)
    first = lax.axis_index("inline") % 2 == 0
    return jnp.where(first, high, low), jnp.where(first, low, high)


def unpack_marks(times, limit, sat, even_in, odd_in, masks, limits):
    lines, cells, depth = sat.shape
    mask_at, limit_at, _ = payload_layout(times, lines)

    def halo(arrived, low):
        row_at = 0 if low else H + cells
        for y in range(lines):
            masks[y, pl.ds(row_at, H), :] = arrived[pl.ds(mask_at + y * H, H), :].astype(jnp.float32)
        value = arrived[pl.ds(limit_at, LIMIT_ROWS), :].astype(jnp.float32)
        for part in range(H // LIMIT_ROWS):
            limits[pl.ds(row_at + part * LIMIT_ROWS, LIMIT_ROWS), :] = value

    by_parity(even_in, odd_in, halo)
    for y in range(lines):
        masks[y, pl.ds(H, cells), :] = (sat[y] != 0).astype(jnp.float32)
    limits[pl.ds(H, cells), :] = jnp.full((cells, depth), limit[0], jnp.int32).astype(jnp.float32)


def unpack_halo(position, shape, even_in, odd_in, low_out, low_at, high_out, high_at):
    times, lines, _, _ = shape

    def halo(arrived, low):
        out, field_at = (low_out, low_at) if low else (high_out, high_at)
        for t in range(times):
            for y in range(lines):
                at = ((position * times + t) * lines + y) * REACH
                out[t, y, pl.ds(field_at, REACH), :] = arrived[pl.ds(at, REACH), :].astype(jnp.float32)

    by_parity(even_in, odd_in, halo)


def image_of(center, far):
    image = center[0] * far[0]
    for c, f in zip(center[1:], far[1:]):
        image = image + c * f
    return image


def accumulate(center, sums, offsets, far_at, masked, mask_at):
    heavy, plain = sums
    times = range(len(center))
    near = {}
    for offset in offsets:
        far = far_at(offset)
        image = masked(image_of(center, far), offset)
        if abs(offset) <= SHARED:
            terms = [image * f for f in far]
            if abs(offset) in near:
                terms = [a + b for a, b in zip(near.pop(abs(offset)), terms)]
            near[abs(offset)] = terms
            if offset == 0 or -offset not in offsets or offset > 0:
                near.pop(abs(offset))
                plain = [plain[t] + terms[t] for t in times]
                if offset:
                    square = square_weight(offset)
                    heavy = [heavy[t] + terms[t] * square for t in times]
        else:
            square = square_weight(offset)
            weighed = image * jnp.where(mask_at(offset) != 0.0, SATURATION * SATURATION, square)
            plain = [plain[t] + image * far[t] for t in times]
            heavy = [heavy[t] + weighed * far[t] for t in times]
    return heavy, plain


def paired(largest, smallest=0):
    return [sign * size for size in range(smallest, largest + 1) for sign in ((-1, 1) if size else (1,))]


def tiles_of(field, y, base):
    times = field.shape[0]
    both = [field[t, y, pl.ds(base, PAIR), :].astype(jnp.float32) for t in range(times)]
    return [[rows[half * ROWS : (half + 1) * ROWS] for rows in both] for half in range(2)]


def inner_kernel(limit, src, rcv, sat, heavy_out, plain_out, shifted, masks):
    times, lines, cells, depth = src.shape
    zero = jnp.zeros((ROWS, depth), jnp.float32)
    blank = jnp.zeros((REACH, depth), jnp.float32)
    for t in range(times):
        for y in range(lines):
            shifted[t, y, pl.ds(0, REACH), :] = blank
            shifted[t, y, pl.ds(REACH, cells), :] = rcv[t, y].astype(jnp.float32)
            shifted[t, y, pl.ds(REACH + cells, REACH), :] = blank
    for y in range(lines):
        masks[y, pl.ds(0, H), :] = blank[:H]
        masks[y, pl.ds(H, cells), :] = (sat[y] != 0).astype(jnp.float32)
        masks[y, pl.ds(H + cells, H), :] = blank[:H]
    inside = [(size <= limit[0]).astype(jnp.float32) for size in range(H + 1)]

    def tile(index, carry):
        base = pl.multiple_of(index * PAIR, PAIR)
        for y in range(lines):
            for half, center in enumerate(tiles_of(src, y, base)):
                at = base + half * ROWS
                heavy, plain = accumulate(
                    center,
                    ([zero] * times, [zero] * times),
                    paired(H),
                    lambda h: [shifted[t, y, pl.ds(at + REACH + 2 * h, ROWS), :] for t in range(times)],
                    lambda image, h: image * inside[abs(h)] if abs(h) > ALWAYS else image,
                    lambda h: masks[y, pl.ds(at + H + h, ROWS), :],
                )
                for t in range(times):
                    heavy_out[t, y, pl.ds(at, ROWS), :] = heavy[t]
                    plain_out[t, y, pl.ds(at, ROWS), :] = plain[t]
        return carry

    lax.fori_loop(0, cells // PAIR, tile, 0)


def within(limits, at):
    def masked(image, offset):
        if abs(offset) <= ALWAYS:
            return image
        return jnp.where(limits[pl.ds(at + H + offset, ROWS), :] >= float(abs(offset)), image, 0.0)

    return masked


def outer_kernel(limit, src, sat, even_in, odd_in, heavy_in, plain_in, heavy, plain, sums, low, high, masks, limits):
    times, lines, cells, depth = src.shape
    unpack_marks(times, limit, sat, even_in, odd_in, masks, limits)
    unpack_halo(1, src.shape, even_in, odd_in, low, 0, high, ROWS)
    blank = jnp.zeros((ROWS, depth), jnp.float32)
    for t in range(times):
        for y in range(lines):
            low[t, y, pl.ds(REACH, ROWS), :] = blank
            high[t, y, pl.ds(0, ROWS), :] = blank

    for group in range(REACH // PAIR):

        def tile(index, carry, group=group):
            for side, shifted in ((0, low), (1, high)):

                @pl.when(index == side)
                def _():
                    first = group * PAIR if side == 0 else cells - (group + 1) * PAIR
                    base = pl.multiple_of(first + (index - side) * PAIR, PAIR)
                    shift = REACH * 0 if side else REACH
                    origin = ROWS - cells if side else 0
                    for y in range(lines):
                        for half, center in enumerate(tiles_of(src, y, base)):
                            at = base + half * ROWS
                            rank = 2 * group + (1 - half if side else half)
                            sizes = range(ROWS // 2 * rank + 1, H + 1)
                            new_heavy, new_plain = accumulate(
                                center,
                                (
                                    [heavy[t, y, pl.ds(at, ROWS), :] for t in range(times)],
                                    [plain[t, y, pl.ds(at, ROWS), :] for t in range(times)],
                                ),
                                [size if side else -size for size in sizes],
                                lambda h: [
                                    shifted[t, y, pl.ds(at + shift + origin + 2 * h, ROWS), :] for t in range(times)
                                ],
                                within(limits, at),
                                lambda h: masks[y, pl.ds(at + H + h, ROWS), :],
                            )
                            for t in range(times):
                                heavy[t, y, pl.ds(at, ROWS), :] = new_heavy[t]
                                plain[t, y, pl.ds(at, ROWS), :] = new_plain[t]

            return carry

        lax.fori_loop(0, 2, tile, 0)

    zero = jnp.zeros((ROWS, depth), jnp.float32)

    def add(index, totals):
        energy, weighted = totals
        base = pl.multiple_of(index * PAIR, PAIR)
        for y in range(lines):
            for half, center in enumerate(tiles_of(src, y, base)):
                rows = pl.ds(base + half * ROWS, ROWS)
                energy = energy + image_of(center, [plain[t, y, rows, :] for t in range(times)])
                weighted = weighted + image_of(center, [heavy[t, y, rows, :] for t in range(times)])
        return energy, weighted

    energy, weighted = lax.fori_loop(0, cells // PAIR, add, (zero, zero))
    sums[0:1, :] = jnp.full((1, depth), jnp.sum(energy), jnp.float32)
    sums[1:2, :] = jnp.full((1, depth), jnp.sum(weighted), jnp.float32)


def piece_kernel(first, limit, src, rcv, sat, even_in, odd_in, heavy_out, plain_out, shifted, masks, limits):
    times, lines, cells, depth = src.shape
    unpack_marks(times, limit, sat, even_in, odd_in, masks, limits)
    unpack_halo(0, src.shape, even_in, odd_in, shifted, 0, shifted, REACH + cells)
    zero = jnp.zeros((ROWS, depth), jnp.float32)
    for t in range(times):
        for y in range(lines):
            shifted[t, y, pl.ds(REACH, cells), :] = src[t, y].astype(jnp.float32)

    def tile(index, carry):
        base = pl.multiple_of(index * PAIR, PAIR)
        for y in range(lines):
            for half, center in enumerate(tiles_of(rcv, y, first + base)):
                at = first + base + half * ROWS
                heavy, plain = accumulate(
                    center,
                    ([zero] * times, [zero] * times),
                    paired(H),
                    lambda h: [shifted[t, y, pl.ds(at + REACH + 2 * h, ROWS), :] for t in range(times)],
                    within(limits, at),
                    lambda h: masks[y, pl.ds(at + H + h, ROWS), :],
                )
                rows = pl.ds(base + half * ROWS, ROWS)
                for t in range(times):
                    heavy_out[t, y, rows, :] = heavy[t]
                    plain_out[t, y, rows, :] = plain[t]
        return carry

    lax.fori_loop(0, heavy_out.shape[2] // PAIR, tile, 0)


def combine_kernel(cell_count, sums, src_heavy, src_plain, *refs):
    pieces, (src_out, rcv_out, semblance_out) = refs[:-3], refs[-3:]
    energy, weighted = sums[0:1, :], sums[1:2, :]
    semblance = weighted / energy
    inverse_rms = 1.0 / jnp.sqrt(energy / cell_count + EPSILON)
    semblance_out[...] = semblance

    def put(out, start, heavy, plain):
        times, lines, count, _ = heavy.shape
        for t in range(times):
            for y in range(lines):
                value = inverse_rms * (heavy[t, y] - semblance * plain[t, y])
                out[t, y, pl.ds(start, count), :] = value.astype(jnp.bfloat16)

    put(src_out, 0, src_heavy, src_plain)
    start = 0
    for heavy, plain in zip(pieces[::2], pieces[1::2]):
        put(rcv_out, start, heavy, plain)
        start += heavy.shape[2]


def exchanges(size):
    even = [(i, i + 1) for i in range(0, size - 1, 2)]
    odd = [(i, i + 1) for i in range(1, size - 1, 2)]
    return [pairs + [(j, i) for i, j in pairs] for pairs in (even, odd)]


def reduction_steps():
    steps = []
    for axis in ("xline", "inline"):
        size = lax.axis_size(axis)
        assert size & (size - 1) == 0
        for bit in range(size.bit_length() - 1):
            steps.append((axis, [(i, i ^ (1 << bit)) for i in range(size)]))
    return steps


def local(source_field, receiver_field, sat_mask, offset_range):
    times, lines, cells, depth = source_field.shape
    size = lax.axis_size("inline")
    grant = pltpu.CompilerParams(vmem_limit_bytes=GRANT)
    image_cells = lines * cells * depth * (2 * H + 1)
    shape = jax.ShapeDtypeStruct
    sums_shape = shape((2, depth), jnp.float32)
    total = shape((times, lines, cells, depth), jnp.float32)
    field_out = shape(source_field.shape, jnp.bfloat16)
    extended = pltpu.VMEM((times, lines, cells + 2 * REACH, depth), jnp.float32)
    edge = pltpu.VMEM((times, lines, ROWS + REACH, depth), jnp.float32)
    masks = pltpu.VMEM((lines, cells + 2 * H, depth), jnp.float32)
    limits = pltpu.VMEM((cells + 2 * H, depth), jnp.float32)

    def cost(share):
        return pl.CostEstimate(flops=int(24 * image_cells * share), bytes_accessed=1 << 20, transcendentals=0)

    src, rcv, sat = source_field, receiver_field, sat_mask
    even, odd = payloads(src, rcv, sat, offset_range)
    even_route, odd_route = exchanges(size)
    odd = lax.ppermute(odd, "inline", odd_route)
    even = lax.ppermute(even, "inline", even_route)

    heavy, plain = pl.pallas_call(
        inner_kernel,
        out_shape=(total, total),
        in_specs=[SMEM] + [VMEM] * 3,
        out_specs=(VMEM, VMEM),
        scratch_shapes=[extended, masks],
        cost_estimate=cost(1),
        compiler_params=grant,
        name="inner",
    )(offset_range, src, rcv, sat)
    heavy, plain, sums = pl.pallas_call(
        outer_kernel,
        out_shape=(total, total, sums_shape),
        in_specs=[SMEM] + [VMEM] * 6,
        out_specs=(VMEM, VMEM, VMEM),
        scratch_shapes=[edge, edge, masks, limits],
        input_output_aliases={5: 0, 6: 1},
        cost_estimate=cost(0.25),
        compiler_params=grant,
        name="outer",
    )(offset_range, src, sat, even, odd, heavy, plain)

    steps = reduction_steps()
    count = cells // PIECES
    piece = shape((times, lines, count, depth), jnp.float32)
    pieces = []
    for number in range(max(len(steps), PIECES)):
        if number < PIECES:
            sums, src, rcv = lax.optimization_barrier((sums, src, rcv))
            latest = pl.pallas_call(
                functools.partial(piece_kernel, number * count),
                out_shape=(piece, piece),
                in_specs=[SMEM] + [VMEM] * 5,
                out_specs=(VMEM, VMEM),
                scratch_shapes=[extended, masks, limits],
                cost_estimate=cost(1 / PIECES),
                compiler_params=grant,
                name="piece",
            )(offset_range, src, rcv, sat, even, odd)
        if number < len(steps):
            sums = sums + lax.ppermute(sums, *steps[number])
        if number < PIECES:
            sums, latest = lax.optimization_barrier((sums, latest))
            pieces += latest

    cell_count = float(lines * lax.axis_size("xline") * cells * size * depth * (2 * H + 1))
    src_adj, rcv_adj, semblance = pl.pallas_call(
        functools.partial(combine_kernel, cell_count),
        out_shape=(field_out, field_out, shape((1, depth), jnp.float32)),
        in_specs=[VMEM] * (3 + len(pieces)),
        out_specs=(VMEM, VMEM, VMEM),
        compiler_params=grant,
        name="combine",
    )(sums, heavy, plain, *pieces)
    return src_adj, rcv_adj, semblance[0, 0]


def solution(mesh):
    return jax.shard_map(
        local,
        mesh=mesh,
        in_specs=(
            P(None, "xline", "inline", None),
            P(None, "xline", "inline", None),
            P("xline", "inline", None),
            P("inline"),
        ),
        out_specs=(P(None, "xline", "inline", None), P(None, "xline", "inline", None), P()),
        check_vma=False,
    )
```

time: 76.5 us -> 35.4 us (0.46)
  blocking collectives: 45.7 us -> 0 us
  starting transfers between devices: 3.6 us -> 12.5 us
  Pallas kernels: 19.7 us -> 12.1 us
  waiting for transfers between devices: 3.3 us -> 7.08 us
  local copies, waits for them, and re-layouts: 1.99 us -> 1.06 us
    all_gather x1 -> x0, blocking collectives: 45.7 us -> none  [local(): gathered = lax.all_gather(sums, ('inline', 'xline'))]
    ppermute x2 -> x7, starting transfers between devices: 3.6 us -> 12.5 us  [the longest x5 6.14 us: local(): sums = sums + lax.ppermute(sums, *steps[number])]
    pallas_call x3 -> x6, Pallas kernels: 17.7 us -> 11.4 us  [the longest x4 5.05 us: local(): pl.pallas_call(functools.partial(piece_kernel, number * count), out_shape...]
    ppermute x2 -> x7, waiting for transfers between devices: 3.3 us -> 7.08 us  [the longest x5 5.4 us: local(): sums = sums + lax.ppermute(sums, *steps[number])]
    unnamed x6, local copies, waits for them, and re-layouts: 1.99 us -> 0.05 us
    pallas_call x1, Pallas kernels: 2.02 us -> 0.76 us  [local(): pl.pallas_call(functools.partial(combine_kernel, cell_count), out_shape=(...]
    slice x0 -> x2, local copies, waits for them, and re-layouts: none -> 0.93 us  [rows(): lax.slice_in_dim(field, start, start + REACH, axis=2).reshape(-1, depth)]
  transfers between devices with their start and end apart: 2 -> 7, of which waited for: 1 -> 5; matrix products, arithmetic and copies ran while one was open for 0% -> 0% of each run, Pallas kernels for 0% -> 28%
where the time goes in v2:
time: 35.4 us; the launch traced here: 35.1 us
  starting transfers between devices  12.5 us (35%)
  Pallas kernels  12.1 us (34%)
  waiting for transfers between devices  7.08 us (20%)
  between operations  1.37 us (4%)
  local copies, waits for them, and re-layouts  1.06 us (3%)
  other arithmetic  0.9 us (3%)
    ppermute x5, starting transfers between devices, local(): sums = sums + lax.ppermute(sums, *steps[number])  6.14 us
    ppermute x1, starting transfers between devices, local(): even = lax.ppermute(even, 'inline', even_route)  5.73 us
    ppermute x5, waiting for transfers between devices, local(): sums = sums + lax.ppermute(sums, *steps[number])  5.4 us
    pallas_call x4, Pallas kernels, local(): pl.pallas_call(functools.partial(piece_kernel, number * count), out_shape...  5.05 us
    pallas_call x1, Pallas kernels, local(): pl.pallas_call(inner_kernel, out_shape=(total, total), in_specs=[SMEM] +...  4.76 us
    ppermute x1, waiting for transfers between devices, local(): even = lax.ppermute(even, 'inline', even_route)  1.68 us
    pallas_call x1, Pallas kernels, local(): pl.pallas_call(outer_kernel, out_shape=(total, total, sums_shape), in_spe...  1.56 us
    slice x2, local copies, waits for them, and re-layouts, rows(): lax.slice_in_dim(field, start, start + REACH, axis=2).reshape(-1, depth)  0.93 us
  transfers between devices with their start and end apart: 7, of which 5 were waited for; matrix products, arithmetic and copies ran while one was open for 0% of the time, Pallas kernels for 28%

profile of v2, /device:TPU:0, one launch (start us, length us, event | category | flops | bytes accessed | tf_op | source)
XLA Modules:
  0.0 35.1 jit_solution(13706499437478758199)
XLA Ops:
  1.3 0.7 %fusion.3 = (bf16[32,128]{1,0:T(8,128)(2,1)S(1)}, bf16[32,128]{1,0:T(8,128)(2,1)S(1)}) fusion(s32[1,128,128]{2,1,0:T(8,128)} %sat.11), kind=kLoop, calls=%fused_computation.9 | loop fusion | flops 16384 | bytes 49152 | tf_op jit(solution)/shard_map/convert_element_type | solution.py:57
  2.0 0.9 %fusion.5 = (bf16[4,1,64,128]{3,2,1,0:T(8,128)(2,1)S(1)}, bf16[4,1,64,128]{3,2,1,0:T(8,128)(2,1)S(1)}) fusion(bf16[4,1,128,128]{3,2,1,0:T(8,128)(2,1)} %rcv.5), kind=kLoop, calls=%fused_computation.11 | loop fusion | bytes 262144 | tf_op jit(solution)/shard_map/slice | solution.py:55
  3.0 0.0 copy-done
  3.0 0.1 pad.7.clone
  3.1 0.1 broadcast_select_fusion
  3.3 0.7 %collective-permute-start.1 = (bf16[560,128]{1,0:T(8,128)(2,1)S(1)}, bf16[560,128]{1,0:T(8,128)(2,1)S(1)}, u32[]{:S(2)}, u32[]{:S(2)}) collective-permute-start(bf16[560,128]{1,0:T(8,128)(2,1)S(1)} %get-tuple-element.83), channel_id=1, source_target_pairs={{2,4},{6,8},{10,12},{14,16},{18,20},{22,24},{26,28},{4,2},{8,6},{1... | collective-permute-start | bytes 430088 | tf_op jit(solution)/shard_map/ppermute | solution.py:336
  3.9 5.7 %collective-permute-start = (bf16[560,128]{1,0:T(8,128)(2,1)S(1)}, bf16[560,128]{1,0:T(8,128)(2,1)S(1)}, u32[]{:S(2)}, u32[]{:S(2)}) collective-permute-start(bf16[560,128]{1,0:T(8,128)(2,1)S(1)} %get-tuple-element.84), channel_id=1, source_target_pairs={{0,2},{4,6},{8,10},{12,14},{16,18},{20,22},{24,26},{28,30},{2,0},{... | collective-permute-start | bytes 430088 | tf_op jit(solution)/shard_map/ppermute | solution.py:337
  9.7 4.8 %inner.1 = (f32[4,1,128,128]{3,2,1,0:T(8,128)S(1)}, f32[4,1,128,128]{3,2,1,0:T(8,128)S(1)}) custom-call(s32[1]{0:T(128)S(6)} %copy.11.limit, bf16[4,1,128,128]{3,2,1,0:T(8,128)(2,1)S(1)} %copy-done, bf16[4,1,128,128]{3,2,1,0:T(8,128)(2,1)S(1)} %copy-done.1, s32[1,128,128]{2,1,0:T(8,128)S(1)} %copy-done.2), custom_call_target="tpu_custom_call" | custom-call | flops 25559040 | bytes 1048576 | tf_op jit(solution)/shard_map/inner/pallas_call | solution.py:339
  14.4 0.0 collective-permute-done.1.odd_in
  14.5 1.7 %collective-permute-done.even_in = bf16[560,128]{1,0:T(8,128)(2,1)S(1)} collective-permute-done((bf16[560,128]{1,0:T(8,128)(2,1)S(1)}, bf16[560,128]{1,0:T(8,128)(2,1)S(1)}, u32[]{:S(2)}, u32[]{:S(2)}) %collective-permute-start) | collective-permute-done | bytes 143392 | tf_op jit(solution)/shard_map/ppermute | solution.py:337
  16.1 1.6 %outer.1 = (f32[4,1,128,128]{3,2,1,0:T(8,128)S(1)}, f32[4,1,128,128]{3,2,1,0:T(8,128)S(1)}, f32[2,128]{1,0:T(2,128)S(1)}) custom-call(s32[1]{0:T(128)S(6)} %copy.11.limit, bf16[4,1,128,128]{3,2,1,0:T(8,128)(2,1)S(1)} %copy-done, s32[1,128,128]{2,1,0:T(8,128)S(1)} %copy-done.2, ...), custom_call_target="tpu_custom_call", output_to_operand_aliasing={{0}: (5, {}), {1}: (6, {})} | custom-call | flops 6389760 | bytes 1048576 | tf_op jit(solution)/shard_map/outer/pallas_call | solution.py:349
  17.7 0.1 collective-permute-start.2
  17.8 1.3 %piece.4 = (f32[4,1,32,128]{3,2,1,0:T(8,128)S(1)}, f32[4,1,32,128]{3,2,1,0:T(8,128)S(1)}) custom-call(s32[1]{0:T(128)S(6)} %copy.11.limit, bf16[4,1,128,128]{3,2,1,0:T(8,128)(2,1)S(1)} %copy-done, bf16[4,1,128,128]{3,2,1,0:T(8,128)(2,1)S(1)} %copy-done.1, s32[1,128,128]{2,1,0:T(8,128)S(1)} %copy-done.2, bf16[560,128]{1,0:T(8,128)(2,1)S(1)} %collective-permute-done.even_in, ...), custom_call_target="tpu_custom_call" | custom-call | flops 6389760 | bytes 1048576 | tf_op jit(solution)/shard_map/piece/pallas_call | solution.py:368
  19.1 1.9 %collective-permute-start.3 = (f32[2,128]{1,0:T(2,128)S(1)}, f32[2,128]{1,0:T(2,128)S(1)}, u32[]{:S(2)}, u32[]{:S(2)}) collective-permute-start(f32[2,128]{1,0:T(2,128)S(1)} %add.20), channel_id=1, source_target_pairs={{0,2},{2,0},{4,6},{6,4},{8,10},{10,8},{12,14},{14,12},{16,18},{18,... | collective-permute-start | bytes 3080 | tf_op jit(solution)/shard_map/ppermute | solution.py:379
  21.0 1.3 %piece.5 = (f32[4,1,32,128]{3,2,1,0:T(8,128)S(1)}, f32[4,1,32,128]{3,2,1,0:T(8,128)S(1)}) custom-call(s32[1]{0:T(128)S(6)} %copy.11.limit, bf16[4,1,128,128]{3,2,1,0:T(8,128)(2,1)S(1)} %copy-done, bf16[4,1,128,128]{3,2,1,0:T(8,128)(2,1)S(1)} %copy-done.1, s32[1,128,128]{2,1,0:T(8,128)S(1)} %copy-done.2, bf16[560,128]{1,0:T(8,128)(2,1)S(1)} %collective-permute-done.even_in, ...), custom_call_target="tpu_custom_call" | custom-call | flops 6389760 | bytes 1048576 | tf_op jit(solution)/shard_map/piece/pallas_call | solution.py:368
  22.2 0.5 %collective-permute-done.3 = f32[2,128]{1,0:T(2,128)S(1)} collective-permute-done((f32[2,128]{1,0:T(2,128)S(1)}, f32[2,128]{1,0:T(2,128)S(1)}, u32[]{:S(2)}, u32[]{:S(2)}) %collective-permute-start.3) | collective-permute-done | bytes 1056 | tf_op jit(solution)/shard_map/ppermute | solution.py:379
  22.7 1.3 %piece.6 = (f32[4,1,32,128]{3,2,1,0:T(8,128)S(1)}, f32[4,1,32,128]{3,2,1,0:T(8,128)S(1)}) custom-call(s32[1]{0:T(128)S(6)} %copy.11.limit, bf16[4,1,128,128]{3,2,1,0:T(8,128)(2,1)S(1)} %copy-done, bf16[4,1,128,128]{3,2,1,0:T(8,128)(2,1)S(1)} %copy-done.1, s32[1,128,128]{2,1,0:T(8,128)S(1)} %copy-done.2, bf16[560,128]{1,0:T(8,128)(2,1)S(1)} %collective-permute-done.even_in, ...), custom_call_target="tpu_custom_call" | custom-call | flops 6389760 | bytes 1048576 | tf_op jit(solution)/shard_map/piece/pallas_call | solution.py:368
  24.0 2.3 %collective-permute-done.4 = f32[2,128]{1,0:T(2,128)S(1)} collective-permute-done((f32[2,128]{1,0:T(2,128)S(1)}, f32[2,128]{1,0:T(2,128)S(1)}, u32[]{:S(2)}, u32[]{:S(2)}) %collective-permute-start.4) | collective-permute-done | bytes 1056 | tf_op jit(solution)/shard_map/ppermute | solution.py:379
  26.3 1.6 %collective-permute-start.5 = (f32[2,128]{1,0:T(2,128)S(1)}, f32[2,128]{1,0:T(2,128)S(1)}, u32[]{:S(2)}, u32[]{:S(2)}) collective-permute-start(f32[2,128]{1,0:T(2,128)S(1)} %add.22), channel_id=1, source_target_pairs={{0,8},{2,10},{4,12},{6,14},{8,0},{10,2},{12,4},{14,6},{16,24},{18,... | collective-permute-start | bytes 3080 | tf_op jit(solution)/shard_map/ppermute | solution.py:379
  27.9 1.3 %piece.7 = (f32[4,1,32,128]{3,2,1,0:T(8,128)S(1)}, f32[4,1,32,128]{3,2,1,0:T(8,128)S(1)}) custom-call(s32[1]{0:T(128)S(6)} %copy.11.limit, bf16[4,1,128,128]{3,2,1,0:T(8,128)(2,1)S(1)} %copy-done, bf16[4,1,128,128]{3,2,1,0:T(8,128)(2,1)S(1)} %copy-done.1, s32[1,128,128]{2,1,0:T(8,128)S(1)} %copy-done.2, bf16[560,128]{1,0:T(8,128)(2,1)S(1)} %collective-permute-done.even_in, ...), custom_call_target="tpu_custom_call" | custom-call | flops 6389760 | bytes 1048576 | tf_op jit(solution)/shard_map/piece/pallas_call | solution.py:368
  29.1 0.7 %collective-permute-done.5 = f32[2,128]{1,0:T(2,128)S(1)} collective-permute-done((f32[2,128]{1,0:T(2,128)S(1)}, f32[2,128]{1,0:T(2,128)S(1)}, u32[]{:S(2)}, u32[]{:S(2)}) %collective-permute-start.5) | collective-permute-done | bytes 1056 | tf_op jit(solution)/shard_map/ppermute | solution.py:379
  29.9 2.6 %collective-permute-start.6 = (f32[2,128]{1,0:T(2,128)S(1)}, f32[2,128]{1,0:T(2,128)S(1)}, u32[]{:S(2)}, u32[]{:S(2)}) collective-permute-start(f32[2,128]{1,0:T(2,128)S(1)} %add.23), channel_id=1, source_target_pairs={{0,16},{2,18},{4,20},{6,22},{8,24},{10,26},{12,28},{14,30},{16,0},... | collective-permute-start | bytes 3080 | tf_op jit(solution)/shard_map/ppermute | solution.py:379
  32.5 1.9 %collective-permute-done.6 = f32[2,128]{1,0:T(2,128)S(1)} collective-permute-done((f32[2,128]{1,0:T(2,128)S(1)}, f32[2,128]{1,0:T(2,128)S(1)}, u32[]{:S(2)}, u32[]{:S(2)}) %collective-permute-start.6) | collective-permute-done | bytes 1056 | tf_op jit(solution)/shard_map/ppermute | solution.py:379
  34.3 0.8 %combine.1 = (bf16[4,1,128,128]{3,2,1,0:T(8,128)(2,1)}, bf16[4,1,128,128]{3,2,1,0:T(8,128)(2,1)}, f32[1,128]{1,0:T(1,128)}) custom-call(f32[2,128]{1,0:T(2,128)S(1)} %add.24.sums, f32[4,1,128,128]{3,2,1,0:T(8,128)S(1)} %get-tuple-element.70.src_heavy, f32[4,1,128,128]{3,2,1,0:T(8,128)S(1)} %get-tuple-element.71.src_plain, ...), custom_call_target="tpu_custom_call" | custom-call | tf_op jit(solution)/shard_map/combine/pallas_call | solution.py:385
  (14 shorter events, 0.0 us)
Async XLA Ops:
  2.0 1.0 %copy-start = (bf16[4,1,128,128]{3,2,1,0:T(8,128)(2,1)S(1)}, bf16[4,1,128,128]{3,2,1,0:T(8,128)(2,1)}, u32[]{:S(2)}) copy-start(bf16[4,1,128,128]{3,2,1,0:T(8,128)(2,1)} %src.7) | copy-start | bytes 393220
  3.1 6.6 %copy-start.1 = (bf16[4,1,128,128]{3,2,1,0:T(8,128)(2,1)S(1)}, bf16[4,1,128,128]{3,2,1,0:T(8,128)(2,1)}, u32[]{:S(2)}) copy-start(bf16[4,1,128,128]{3,2,1,0:T(8,128)(2,1)} %rcv.5) | copy-start | bytes 393220
  3.1 6.6 %copy-start.2 = (s32[1,128,128]{2,1,0:T(8,128)S(1)}, s32[1,128,128]{2,1,0:T(8,128)}, u32[]{:S(2)}) copy-start(s32[1,128,128]{2,1,0:T(8,128)} %sat.11) | copy-start | bytes 196612
  3.3 11.2 %collective-permute-start.1 = (bf16[560,128]{1,0:T(8,128)(2,1)S(1)}, bf16[560,128]{1,0:T(8,128)(2,1)S(1)}, u32[]{:S(2)}, u32[]{:S(2)}) collective-permute-start(bf16[560,128]{1,0:T(8,128)(2,1)S(1)} %get-tuple-element.83), channel_id=1, source_target_pairs={{2,4},{6,8},{10,12},{14,16},{18,20},{22,24},{26,28},{4,2},{8,6},{1... | collective-permute-start | bytes 430088 | tf_op jit(solution)/shard_map/ppermute | solution.py:336
  3.9 12.2 %collective-permute-start = (bf16[560,128]{1,0:T(8,128)(2,1)S(1)}, bf16[560,128]{1,0:T(8,128)(2,1)S(1)}, u32[]{:S(2)}, u32[]{:S(2)}) collective-permute-start(bf16[560,128]{1,0:T(8,128)(2,1)S(1)} %get-tuple-element.84), channel_id=1, source_target_pairs={{0,2},{4,6},{8,10},{12,14},{16,18},{20,22},{24,26},{28,30},{2,0},{... | collective-permute-start | bytes 430088 | tf_op jit(solution)/shard_map/ppermute | solution.py:337
  17.7 1.4 %collective-permute-start.2 = (f32[2,128]{1,0:T(2,128)S(1)}, f32[2,128]{1,0:T(2,128)S(1)}, u32[]{:S(2)}, u32[]{:S(2)}) collective-permute-start(f32[2,128]{1,0:T(2,128)S(1)} %get-tuple-element.46), channel_id=1, source_target_pairs={{0,1},{1,0},{2,3},{3,2},{4,5},{5,4},{6,7},{7,6},{8,9},{9,8},{10,11... | collective-permute-start | bytes 3080 | tf_op jit(solution)/shard_map/ppermute | solution.py:379
  19.1 3.6 %collective-permute-start.3 = (f32[2,128]{1,0:T(2,128)S(1)}, f32[2,128]{1,0:T(2,128)S(1)}, u32[]{:S(2)}, u32[]{:S(2)}) collective-permute-start(f32[2,128]{1,0:T(2,128)S(1)} %add.20), channel_id=1, source_target_pairs={{0,2},{2,0},{4,6},{6,4},{8,10},{10,8},{12,14},{14,12},{16,18},{18,... | collective-permute-start | bytes 3080 | tf_op jit(solution)/shard_map/ppermute | solution.py:379
  22.7 3.6 %collective-permute-start.4 = (f32[2,128]{1,0:T(2,128)S(1)}, f32[2,128]{1,0:T(2,128)S(1)}, u32[]{:S(2)}, u32[]{:S(2)}) collective-permute-start(f32[2,128]{1,0:T(2,128)S(1)} %add.21), channel_id=1, source_target_pairs={{0,4},{2,6},{4,0},{6,2},{8,12},{10,14},{12,8},{14,10},{16,20},{18,... | collective-permute-start | bytes 3080 | tf_op jit(solution)/shard_map/ppermute | solution.py:379
  26.3 3.6 %collective-permute-start.5 = (f32[2,128]{1,0:T(2,128)S(1)}, f32[2,128]{1,0:T(2,128)S(1)}, u32[]{:S(2)}, u32[]{:S(2)}) collective-permute-start(f32[2,128]{1,0:T(2,128)S(1)} %add.22), channel_id=1, source_target_pairs={{0,8},{2,10},{4,12},{6,14},{8,0},{10,2},{12,4},{14,6},{16,24},{18,... | collective-permute-start | bytes 3080 | tf_op jit(solution)/shard_map/ppermute | solution.py:379
  29.9 4.5 %collective-permute-start.6 = (f32[2,128]{1,0:T(2,128)S(1)}, f32[2,128]{1,0:T(2,128)S(1)}, u32[]{:S(2)}, u32[]{:S(2)}) collective-permute-start(f32[2,128]{1,0:T(2,128)S(1)} %add.23), channel_id=1, source_target_pairs={{0,16},{2,18},{4,20},{6,22},{8,24},{10,26},{12,28},{14,30},{16,0},... | collective-permute-start | bytes 3080 | tf_op jit(solution)/shard_map/ppermute | solution.py:379
